TPU v7x, 128 devices: a whole 4x4x4 slice. The times are simulated.
128 devices in a mesh: dp: 16 (over x, y_lo, core), vocab: 8 (over y_hi, z).
Axes of the slice: x: 4, y: 4 (y_hi: 2, y_lo: 2; y = y_hi * 2 + y_lo), z: 4, core: 2. Of those that a mesh axis runs over, the one named last changes fastest.
Arguments:
- hidden: bfloat16 [2048, 3584], P('dp'), may hold values from -256 to 256
- head_weight: bfloat16 [3584, 131072], P(None, ('dp', 'vocab')), may hold values from -0.3125 to 0.3125
- teacher_logits: bfloat16 [2048, 16, 8192], P('dp', None, 'vocab'), may hold values from -80 to 160
- upstream: float32 [2048], replicated, may hold values from 2000 to 20000
Outputs:
- grad_hidden: bfloat16 [2048, 3584], P('dp', 'vocab')
- grad_weight: bfloat16 [3584, 131072], P(None, ('dp', 'vocab'))
- kl_rows: float32 [2048], P('dp')
All inputs are finite; a program needn't handle non-finite values.
Results may differ from a plain program's by a relative error of at most 0.018.
Values may be sent and summed in bfloat16 or wider, within the bound.
A program may use at most 192 MiB of HBM per device.

v0:
```python
import jax
import jax.numpy as jnp
from jax import lax
from jax.sharding import PartitionSpec as P


def local(hidden, head_weight, teacher_logits, upstream):
    rows_local = hidden.shape[0]
    columns = head_weight.shape[1]
    gathered = lax.all_gather(hidden, "dp", axis=0, tiled=True)
    total_rows = gathered.shape[0]
    student = jnp.dot(gathered, head_weight, preferred_element_type=jnp.float32)
    received = lax.all_to_all(teacher_logits, "dp", split_axis=1, concat_axis=0, tiled=True)
    teacher = received.reshape(total_rows, columns).astype(jnp.float32)
    local_s = jnp.max(student, axis=1)
    local_t = jnp.max(teacher, axis=1)
    peak_s, peak_t = lax.pmax((local_s, local_t), ("dp", "vocab"))
    expo_t = jnp.exp(teacher - peak_t[:, None])
    total_s, total_t, cross = lax.psum(
        (
            jnp.sum(jnp.exp(student - peak_s[:, None]), axis=1),
            jnp.sum(expo_t, axis=1),
            jnp.sum(expo_t * (teacher - student), axis=1),
        ),
        ("dp", "vocab"),
    )
    lse_s = peak_s + jnp.log(total_s)
    lse_t = peak_t + jnp.log(total_t)
    kl_all = cross / total_t - lse_t + lse_s
    grad_logits = (
        upstream[:, None] * (jnp.exp(student - lse_s[:, None]) - jnp.exp(teacher - lse_t[:, None]))
    ).astype(jnp.bfloat16)
    grad_weight = lax.dot_general(
        gathered, grad_logits, (((0,), (0,)), ((), ())), preferred_element_type=jnp.float32
    ).astype(jnp.bfloat16)
    row_part = lax.psum_scatter(
        lax.dot_general(
            grad_logits, head_weight, (((1,), (1,)), ((), ())), preferred_element_type=jnp.float32
        ).astype(jnp.bfloat16),
        "dp",
        scatter_dimension=0,
        tiled=True,
    )
    grad_hidden = lax.psum_scatter(row_part, "vocab", scatter_dimension=1, tiled=True).astype(
        jnp.float32
    )
    kl_rows = lax.dynamic_slice_in_dim(kl_all, lax.axis_index("dp") * rows_local, rows_local, 0)
    return (grad_hidden.astype(jnp.bfloat16), grad_weight, kl_rows)


def solution(mesh):
    return jax.shard_map(
        local,
        mesh=mesh,
        in_specs=(P("dp", None), P(None, ("dp", "vocab")), P("dp", None, "vocab"), P()),
        out_specs=(P("dp", "vocab"), P(None, ("dp", "vocab")), P("dp")),
        check_vma=False,
    )
```

profile of v0, /device:TPU:2, one launch (start us, length us, event | category | flops | bytes accessed | tf_op | source)
XLA Modules:
  0.0 567.9 jit_solution(6361384117321604416)
XLA Ops:
  7.2 0.0 all-gather.2.cloned.1.call-start
  7.2 0.7 all-gather.2.cloned.1.call-update
  7.9 0.0 reduce-scatter.5.cloned.1.call-start
  7.9 4.5 copy.28
  12.5 89.6 %all_to_all.15 = bf16[128,16,1024]{2,0,1:T(8,128)(2,1)S(1)} all-to-all(bf16[128,16,1024]{2,0,1:T(8,128)(2,1)S(1)} %copy.28), channel_id=1, replica_groups=mesh['dp'=16,'vocab'=8] {'dp'}, dimensions={1} | all-to-all | bytes 8388608 | tf_op jit(solution)/shard_map/all_to_all | solution.py:13
  102.0 0.0 copy-start
  102.0 2.0 copy-done
  104.0 4.4 bitcast_convert_fusion
  108.4 9.2 %copy.36 = f32[2048,1024]{0,1:T(8,128)} copy(f32[2048,1024]{1,0:T(8,128)} %bitcast.23) | data formatting | bytes 16777216 | tf_op jit(solution)/shard_map/convert_element_type | solution.py:14
  117.6 2.9 bitcast_reduce_fusion
  120.6 15.7 %all-gather.2.cloned.1.call-done = bf16[2048,3584]{1,0:T(8,128)(2,1)} async-done(((bf16[128,3584]{1,0:T(8,128)(2,1)}), bf16[2048,3584]{1,0:T(8,128)(2,1)}) %all-gather.2.cloned.1.call-update) | async-done | bytes 14680080 | tf_op jit(solution)/shard_map/all_gather | solution.py:10
  136.2 21.6 %fusion.1 = (f32[2048]{0:T(1024)S(1)}, f32[2048,1024]{0,1:T(8,128)}) fusion(bf16[2048,3584]{1,0:T(8,128)(2,1)} %all-gather.2.cloned.1.call-done, bf16[3584,1024]{1,0:T(8,128)(2,1)} %param.5), kind=kOutput, calls=%fused_computation.15 | convolution fusion | flops 15034480640 | bytes 30416896 | tf_op jit(solution)/shard_map/dot_general | solution.py:12
  157.9 67.2 %all-reduce.1 = (f32[2048]{0:T(1024)S(1)}, f32[2048]{0:T(1024)S(1)}) all-reduce(f32[2048]{0:T(1024)S(1)} %bitcast_convert_fusion.1, f32[2048]{0:T(1024)S(1)} %get-tuple-element.25), channel_id=1, replica_groups=mesh['dp'=16,'vocab'=8] {'dp','vocab'}, use_global_device_ids=true, to_apply=%region_5.0 | all-reduce | flops 4096 | bytes 32768 | tf_op jit(solution)/shard_map/pmax | solution.py:17
  225.1 0.0 copy-start.1
  225.1 0.0 copy-start.3
  225.1 7.4 %multiply_reduce_fusion = (f32[2048]{0:T(1024)S(1)}, f32[2048]{0:T(1024)S(1)}) fusion(f32[2048,1024]{0,1:T(8,128)} %copy.36, f32[2048,1024]{0,1:T(8,128)} %get-tuple-element.26, f32[2048]{0:T(1024)S(1)} %get-tuple-element.23, f32[2048]{0:T(1024)S(1)} %get-tuple-element.24), kind=kLoop, calls=%fused_computation.1 | loop fusion | flops 12578816 | bytes 16809984 | tf_op jit(solution)/shard_map/reduce_sum | solution.py:23
  232.5 0.0 copy-done.1
  232.5 1.8 exponential_reduce_fusion
  234.3 63.8 %all-reduce = (f32[2048]{0:T(1024)S(1)}, f32[2048]{0:T(1024)S(1)}, f32[2048]{0:T(1024)S(1)}) all-reduce(f32[2048]{0:T(1024)S(1)} %bitcast.26, f32[2048]{0:T(1024)S(1)} %get-tuple-element.19, f32[2048]{0:T(1024)S(1)} %get-tuple-element.18), channel_id=1, replica_groups=mesh['dp'=16,'vocab'=8] {'dp','vocab'}, use_global_device_ids=true, to_apply=%region_7.0 | all-reduce | flops 6144 | bytes 49152 | tf_op jit(solution)/shard_map/psum | solution.py:19
  298.1 0.0 copy-done.3
  298.1 7.1 %multiply_convert_fusion = bf16[2048,1024]{0,1:T(8,128)(2,1)S(1)} fusion(f32[2048,1024]{0,1:T(8,128)} %copy.36, f32[2048,1024]{0,1:T(8,128)} %get-tuple-element.26, f32[2048]{0:T(1024)S(1)} %get-tuple-element.27, f32[2048]{0:T(1024)S(1)} %get-tuple-element.28, f32[2048]{0:T(1024)S(1)} %copy-done.3), kind=kLoop, calls=%fused_computation.2 | loop fusion | flops 10485760 | bytes 20996096 | tf_op jit(solution)/shard_map/convert_element_type | solution.py:32
  305.3 0.0 copy-start.2
  305.3 2.0 copy-done.2
  307.3 21.0 %convolution_convert_fusion = bf16[2048,3584]{1,0:T(8,128)(2,1)} fusion(bf16[2048,1024]{0,1:T(8,128)(2,1)S(1)} %multiply_convert_fusion, bf16[3584,1024]{1,0:T(8,128)(2,1)} %param.5), kind=kOutput, calls=%fused_computation | convolution fusion | flops 15039725568 | bytes 26214400 | tf_op jit(solution)/shard_map/dot_general | solution.py:37
  328.3 0.0 reduce-scatter.5.cloned.1.call-update
  328.4 0.3 reduce-scatter.7.cloned.1.call-start
  328.6 152.2 %reduce-scatter.5.cloned.1.call-done = bf16[128,3584]{1,0:T(8,128)(2,1)} async-done(((bf16[2048,3584]{1,0:T(8,128)(2,1)}), bf16[128,3584]{1,0:T(8,128)(2,1)}) %reduce-scatter.5.cloned.1.call-update) | async-done | bytes 917520 | tf_op jit(solution)/shard_map/reduce_scatter | solution.py:36
  480.9 2.2 copy.37
  483.1 0.0 reduce-scatter.7.cloned.1.call-update
  483.1 21.8 %fusion = bf16[3584,1024]{0,1:T(8,128)(2,1)} fusion(bf16[2048,1024]{0,1:T(8,128)(2,1)} %copy-done.2, bf16[2048,3584]{1,0:T(8,128)(2,1)} %all-gather.2.cloned.1.call-done), kind=kOutput, calls=%fused_computation.6 | convolution fusion | flops 15036055552 | bytes 26214400 | tf_op jit(solution)/shard_map/dot_general | solution.py:33
  504.8 10.4 %copy.35 = bf16[3584,1024]{1,0:T(8,128)(2,1)} copy(bf16[3584,1024]{0,1:T(8,128)(2,1)} %fusion) | data formatting | bytes 14680064
  515.3 0.6 dynamic-slice_add_fusion
  515.9 45.5 %reduce-scatter.7.cloned.1.call-done = bf16[448,128]{1,0:T(8,128)(2,1)} async-done(((bf16[3584,128]{1,0:T(8,128)(2,1)}), bf16[448,128]{1,0:T(8,128)(2,1)}) %reduce-scatter.7.cloned.1.call-update) | async-done | bytes 114704
  (2 shorter events, 0.0 us)
Async XLA Ops:
  7.2 129.1 %all-gather.2.cloned.1.call-start = ((), (), s32[]{:S(2)}) async-start(), calls=%async_computation.3 | async-start | bytes 15597568 | tf_op jit(solution)/shard_map/all_gather | solution.py:10
  7.9 473.0 %reduce-scatter.5.cloned.1.call-start = ((), (), s32[]{:S(2)}) async-start(), calls=%async_computation.4 | async-start | bytes 15597568 | tf_op jit(solution)/shard_map/reduce_scatter | solution.py:36
  102.0 2.0 copy-start
  225.1 7.4 %copy-start.1 = (bf16[128,16,1024]{2,0,1:T(8,128)(2,1)S(1)}, bf16[128,16,1024]{2,0,1:T(8,128)(2,1)}, u32[]{:S(2)}) copy-start(bf16[128,16,1024]{2,0,1:T(8,128)(2,1)} %copy-done) | copy-start | bytes 12582916
  225.1 73.0 %copy-start.3 = (f32[2048]{0:T(1024)S(1)}, f32[2048]{0:T(1024)}, u32[]{:S(2)}) copy-start(f32[2048]{0:T(1024)} %param.7) | copy-start | bytes 24580
  305.3 2.0 copy-start.2
  328.4 233.0 %reduce-scatter.7.cloned.1.call-start = ((), (), s32[]{:S(2)}) async-start(), calls=%async_computation.5 | async-start | bytes 1032192
Sparse Core Ops, SparseCore 0:
  9.7 126.4 all-gather.1
  328.5 152.3 reduce-scatter.4
  485.0 76.3 reduce-scatter.6
where the time goes:
time: 569 us; the launch traced here: 568 us
  blocking collectives  221 us (39%)
  waiting for transfers between devices  214 us (38%)
  matrix products  64.4 us (11%)
  local copies, waits for them, and re-layouts  30.4 us (5%)
  other arithmetic  24.2 us (4%)
  between operations  13.8 us (2%)
    reduce_scatter x1, waiting for transfers between devices, local(): lax.psum_scatter(lax.dot_general(grad_logits, head_weight, (((1,), (1,)),...  152 us
    all_to_all x1, blocking collectives, local(): lax.all_to_all(teacher_logits, 'dp', split_axis=1, concat_axis=0, tiled=T...  89.6 us
    pmax x1, blocking collectives, local(): peak_s, peak_t = lax.pmax((local_s, local_t), ('dp', 'vocab'))  67.2 us
    psum x1, blocking collectives, local(): lax.psum((jnp.sum(jnp.exp(student - peak_s[:, None]), axis=1), jnp.sum(ex...  63.8 us
    unnamed x4, waiting for transfers between devices  46.3 us
    dot_general x1, matrix products, local(): lax.dot_general(gathered, grad_logits, (((0,), (0,)), ((), ())), preferre...  21.8 us
    dot_general x1, matrix products, local(): student = jnp.dot(gathered, head_weight, preferred_element_type=jnp.float32)  21.6 us
    unnamed x11, local copies, waits for them, and re-layouts  21.2 us
  transfers between devices with their start and end apart: 3, of which 3 were waited for; matrix products, arithmetic and copies ran while one was open for 9% of the time, Pallas kernels for 0%

commit v1 on v0

v1 whole, which is shorter than its diff:
```python
import jax
import jax.numpy as jnp
from jax import lax
from jax.experimental import pallas as pl
from jax.experimental.pallas import tpu as pltpu
from jax.sharding import PartitionSpec as P

D = 3584
F = 448
C = 1024
BF = jnp.bfloat16
F32 = jnp.float32
MESH = pl.DeviceIdType.MESH
START = (0, 128, 288)
COUNT = (128, 160, 160)
HALF = (64, 80, 80)


def m4(a):
    return (a + 8) % 4


def dot(a, b, dims):
    return lax.dot_general(a, b, (dims, ((), ())), preferred_element_type=F32)


def loop(n, f):
    def body(i, carry):
        f(i)
        return carry

    lax.fori_loop(0, n, body, 0)


def kernel(hid, w, t_in, up, gh_out, gw_out, kl_out, H, HO, W2, T, S, GX, SB, RA0, RA1, RA2, RB0, RB1, RB2, RC0, RC1,
           RC2, RD, PM, PS, ST, SR, CT, CR, LSE, FIN, stage, s_loc, s_in, s_x, s_y0, s_y, s_yb, s_z, s_f, s_a, s_w, s_h, s_g,
           s_st, s_ct, s_r0, s_r1, s_c0, s_c1, s_c2, s_rd, s_out, s_free):
    d = lax.axis_index("dp")
    v = lax.axis_index("vocab")
    x = d // 4
    p = (d // 2) % 2
    c = d % 2
    yh = v // 4
    y = yh * 2 + p
    z = v % 4
    me = (x, y, z)

    def dev(xx, yy, zz, cc):
        return (xx * 4 + (yy % 2) * 2 + cc, (yy // 2) * 4 + zz)

    def along(axis, k):
        at = [x, y, z]
        at[axis] = m4(at[axis] + k)
        return dev(*at, c)

    sibling = dev(x, y, z, 1 - c)
    yn = m4(y - 1 + 2 * p)
    yl = y + 1 - 2 * p
    dyn = dev(x, yn, z, c)
    dyl = dev(x, yl, z, c)
    xt = [m4(x + 1), m4(x - 1), m4(x + 2)]
    xq = [m4(x - 1), m4(x + 1), m4(x + 2)]
    xk = [m4(x + 2), m4(x + 1), m4(x - 1), x]
    dz = [along(2, 1), along(2, -1)]
    zq = [m4(z - 1), m4(z + 1)]
    a2a = [(x, yl), (xt[2], y), (xt[0], yl), (xt[1], y), (xt[2], yl), (xt[0], y), (xt[1], yl)]
    da = [dev(a, b, z, c) for a, b in a2a]

    partners = [along(a, k) for a in range(3) for k in (1, 2, 3)] + [sibling, da[2], da[4], da[6]]
    barrier = pltpu.get_barrier_semaphore()
    for to in partners:
        pl.semaphore_signal(barrier, inc=1, device_id=to, device_id_type=MESH)
    pl.semaphore_wait(barrier, len(partners))

    def send(src, dst, sems, at, to):
        return pltpu.make_async_remote_copy(
            src_ref=src, dst_ref=dst, send_sem=sems.at[(0, *at)], recv_sem=sems.at[(1, *at)],
            device_id=to, device_id_type=MESH)

    own = pl.ds(pl.multiple_of(z * 32, 32), 32)
    cols_c = pl.ds(pl.multiple_of(c * C, C), C)
    X = [send(hid.at[own], H.at[x, p, z], s_x, (i,), along(0, (1, -1, 2)[i])) for i in range(3)]
    A = [send(HO.at[a, b % 2, :, :, 0:2 * C], T.at[x, p], s_a, (k,), da[k]) for k, (a, b) in enumerate(a2a)]
    Y0 = [send(hid.at[pl.ds(pl.multiple_of(m4(z + k) * 32, 32), 32)], H.at[x, p, m4(z + k)], s_y0, (k,), dyn)
          for k in range(4)]
    low, high = pl.ds(0, 16), pl.ds(16, 16)
    Y1 = [send(H.at[xq[i], p, z], H.at[xq[i], p, z], s_y, (i,), dyn) for i in range(2)]
    Y1.append(send(H.at[xq[2], p, z, high], H.at[xq[2], p, z, high], s_y, (2,), dyn))
    YB = [send(H.at[xq[2], p, zz, low], H.at[xq[2], p, zz, low], s_yb, (k,), dyn)
          for k, zz in enumerate((z, zq[0], zq[1], m4(z + 2)))]
    pairs = [(2, 0), (0, 0), (1, 0), (0, 1), (1, 1), (2, 1)]

    def piece(i, q, zz):
        at = H.at[xq[i], (p + q) % 2, zz]
        return at.at[high] if (i, q) == (2, 1) else at

    def part_of(i, q, zz, r):
        if (i, q) == (2, 1):
            return H.at[xq[i], (p + q) % 2, zz, high, r * (D // 2):(r + 1) * (D // 2)]
        return H.at[xq[i], (p + q) % 2, zz, pl.ds(16 * r, 16)]

    Z = {(i, q): [send(piece(i, q, z), piece(i, q, z), s_z, (i, q, r), dz[r]) for r in range(2)] for i, q in pairs}
    FW = {(i, q): [send(part_of(i, q, zq[r], r), part_of(i, q, zq[r], r), s_f, (i, q, r), dz[r]) for r in range(2)]
          for i, q in pairs}
    WC = send(w, W2.at[:, cols_c], s_w, (), sibling)
    local = [pltpu.make_async_copy(hid.at[pl.ds(32 * k, 32)], H.at[x, p, k], s_loc.at[k]) for k in range(4)]
    local.append(pltpu.make_async_copy(w, W2.at[:, cols_c], s_loc.at[4]))
    for e in X:
        e.start()
    Y0[0].start()

    def t_copy(n, slot):
        return pltpu.make_async_copy(
            t_in.at[pl.ds(pl.multiple_of(n * 256, 256), 256)], stage.at[slot, 0:256], s_in.at[slot])

    t_copy(0, 0).start()
    t_copy(1, 1).start()
    row = lax.broadcasted_iota(jnp.int32, (256, 256), 0)
    col = lax.broadcasted_iota(jnp.int32, (256, 256), 1)
    swap = jnp.where(((row >> 4) == (col & 15)) & ((row & 15) == (col >> 4)), 1.0, 0.0).astype(BF)
    for n in range(8):
        t_copy(n, n % 2).wait()
        moved = jnp.dot(swap, stage[n % 2, 0:256], preferred_element_type=F32).astype(BF)
        if n < 6:
            t_copy(n + 2, n % 2).start()
        for a in range(16):
            HO[a // 4, (a // 2) % 2, n // 2, pl.ds((n % 2) * 16, 16), pl.ds((a % 2) * C, C)] = moved[a * 16:a * 16 + 16]
    WC.start()
    for l in local:
        l.start()
    local.append(pltpu.make_async_copy(HO.at[x, p, :, :, 0:2 * C], T.at[x, p], s_loc.at[5]))
    local[5].start()
    for i in range(3):
        X[i].wait_recv()
        Y1[i].start()
        if i == 2:
            YB[0].start()
        for r in range(2):
            Z[i, 0][r].start()
    for e in A:
        e.start()
    for k in range(1, 4):
        Y0[k].start()

    def teacher(i):
        rows = pl.ds(pl.multiple_of(i * 32, 32), 32)

        def top_of(e, top):
            for g in range(16):
                top = jnp.maximum(top, HO[e // 2, e % 2, i, :, g * 128:(g + 1) * 128].astype(F32))
            return top

        top = lax.fori_loop(0, 8, top_of, jnp.full((32, 128), -1e30, F32))

        def total_of(e, total):
            for g in range(16):
                total = total + jnp.exp(HO[e // 2, e % 2, i, :, g * 128:(g + 1) * 128].astype(F32) - top)
            return total

        FIN[0, rows] = top
        FIN[1, rows] = lax.fori_loop(0, 8, total_of, jnp.zeros((32, 128), F32))

    def merge(top, total):
        top, total = top.T, total.T
        peak = jnp.max(top, axis=0, keepdims=True)
        return peak, jnp.sum(total * jnp.exp(top - peak), axis=0, keepdims=True)

    ST[0, 2] = jnp.full((8, 128), -1e30, F32)
    ST[0, 3] = jnp.zeros((8, 128), F32)
    for i in range(3):
        Y1[i].wait_recv()
        for r in range(2):
            Z[i, 1][r].start()
    loop(4, teacher)
    peak_t, total_t = merge(FIN[0], FIN[1])
    ST[0, 2, pl.ds(x * 2 + p, 1), :] = peak_t
    ST[0, 3, pl.ds(x * 2 + p, 1), :] = total_t
    for l in local[:5]:
        l.wait()
    Y0[0].wait_recv()
    YB[0].wait_recv()
    WC.wait_recv()

    def student(zz):
        def tile(n):
            k = pl.ds(pl.multiple_of(n * C, C), C)
            out = jnp.dot(H[:, :, zz].reshape(256, D), W2[:, k], preferred_element_type=F32)
            S[:, :, zz, :, k] = out.reshape(4, 2, 32, C)

        loop(2, tile)

        def stats(b, carry):
            xx, pp = b // 2, b % 2
            top = S[xx, pp, zz, :, 0:128]
            for g in range(1, 16):
                top = jnp.maximum(top, S[xx, pp, zz, :, g * 128:(g + 1) * 128])
            total = jnp.zeros((32, 128), F32)
            for g in range(16):
                total = total + jnp.exp(S[xx, pp, zz, :, g * 128:(g + 1) * 128] - top)
            PM[xx, pp, zz] = top
            PS[xx, pp, zz] = total
            return carry

        lax.fori_loop(0, 8, stats, 0)

    student(z)
    for i, q in pairs:
        for r in range(2):
            Z[i, q][r].wait_recv()
            if (i, q) == (2, 0):
                YB[1 + r].start()
            FW[i, q][r].start()
        if (i, q) == (1, 0):
            for r in range(2):
                FW[2, 0][r].wait_recv()
            YB[3].start()
    for k in range(1, 4):
        Y0[k].wait_recv()
    for r in range(2):
        YB[1 + r].wait_recv()
        student(zq[r])
    for i, q in pairs[1:]:
        for r in range(2):
            FW[i, q][r].wait_recv()
    YB[3].wait_recv()
    student(m4(z + 2))

    def merge_student(b, carry):
        xx, pp = b // 2, b % 2
        peak, total = merge(PM[xx, pp].reshape(128, 128), PS[xx, pp].reshape(128, 128))
        ST[0, 0, pl.ds(b, 1), :] = peak
        ST[0, 1, pl.ds(b, 1), :] = total
        return carry

    lax.fori_loop(0, 8, merge_student, 0)

    for a in range(3):
        ex = [send(ST.at[a], SR.at[a, k], s_st, (a, k), along(a, k + 1)) for k in range(3)]
        for e in ex:
            e.start()
        for e in (X + Y0 + Y1 + YB + [WC], [e for at in pairs[:3] for e in Z[at] + FW[at]],
                  [e for at in pairs[3:] for e in Z[at] + FW[at]])[a]:
            e.wait_send()
        for e in ex:
            e.wait()
        for s in range(2):
            tops = [ST[a, 2 * s]] + [SR[a, k, 2 * s] for k in range(3)]
            sums = [ST[a, 2 * s + 1]] + [SR[a, k, 2 * s + 1] for k in range(3)]
            peak = jnp.maximum(jnp.maximum(tops[0], tops[1]), jnp.maximum(tops[2], tops[3]))
            total = sum(u * jnp.exp(t - peak) for t, u in zip(tops, sums))
            ST[a + 1, 2 * s] = peak
            ST[a + 1, 2 * s + 1] = total
    LSE[0] = ST[3, 0] + jnp.log(ST[3, 1])
    LSE[1] = ST[3, 2] + jnp.log(ST[3, 3])

    def grads(b):
        def spread(row):
            return jnp.broadcast_to(row, (128, 128)).T

        FIN[0] = spread(LSE[0, pl.ds(b, 1), :])
        FIN[1] = spread(LSE[1, pl.ds(b, 1), :])
        FIN[2] = spread(up[pl.ds(2 * b + c, 1), :])
        xx, pp = b // 2, b % 2

        def part(i):
            rows = pl.ds(pl.multiple_of(i * 32, 32), 32)
            ls, lt, u = FIN[0, rows], FIN[1, rows], FIN[2, rows]
            cross = jnp.zeros((32, 128), F32)
            for g in range(16):
                at = slice(g * 128, (g + 1) * 128)
                s = S[xx, pp, i, :, at]
                t = T[xx, pp, i, :, at].astype(F32)
                pt = jnp.exp(t - lt)
                cross = cross + pt * (t - s)
                T[xx, pp, i, :, at] = (u * (jnp.exp(s - ls) - pt)).astype(BF)
            FIN[3, rows] = cross

        loop(4, part)
        CT[0, pl.ds(b, 1), :] = jnp.sum(FIN[3].T, axis=0, keepdims=True)

    def units(xx):
        def half(n):
            hh = (1 - yh + n // 2) % 2
            feat = pl.ds(pl.multiple_of((hh * 4 + n % 2 * 2) * F, 2 * F), 2 * F)
            out = dot(W2[feat, :], T[xx].reshape(256, 2 * C), ((1,), (1,))).astype(BF)
            for i in range(2):
                SB[xx, 2 * hh, n % 2 * 2 + i] = out[i * F:(i + 1) * F, 0:128]
                SB[xx, 2 * hh + 1, n % 2 * 2 + i] = out[i * F:(i + 1) * F, 128:256]

        loop(4, half)

    RA, RB = (RA0, RA1, RA2), (RB0, RB1, RB2)
    first = [pl.ds(START[o], HALF[o]) for o in range(3)]
    second = [pl.ds(START[o] + HALF[o], COUNT[o] - HALF[o]) for o in range(3)]
    whole = [pl.ds(START[o], COUNT[o]) for o in range(3)]
    lo = [pl.ds(0, HALF[o]) for o in range(3)]
    hi = [pl.ds(HALF[o], COUNT[o] - HALF[o]) for o in range(3)]

    def plus_into(dst, i, *terms):
        total = dst[i].astype(F32)
        for ref, j in terms:
            total = total + ref[j].astype(F32)
        dst[i] = total.astype(BF)

    far0 = [send(SB.at[xk[0], :, :, first[0]], RB0.at[:, :, lo[0]], s_r0, (0,), along(0, 1)),
            send(SB.at[xk[0], :, :, second[0]], RB0.at[:, :, hi[0]], s_r0, (1,), along(0, -1))]
    near0 = [send(SB.at[xk[1], :, :, second[0]], RA0.at[0, :, :, hi[0]], s_r0, (2,), along(0, 1)),
             send(SB.at[xk[2], :, :, first[0]], RA0.at[1, :, :, lo[0]], s_r0, (3,), along(0, -1))]
    relay0 = [send(RB0.at[:, :, lo[0]], RA0.at[0, :, :, lo[0]], s_r0, (4,), along(0, 1)),
              send(RB0.at[:, :, hi[0]], RA0.at[1, :, :, hi[0]], s_r0, (5,), along(0, -1))]
    P2_0 = [send(SB.at[x, m4(y + j), :, whole[0]], RC0.at[j - 1], s_c0, (j - 1,), along(1, j)) for j in (2, 1, 3)]
    P3_0 = [send(SB.at[x, y, m4(z + j), whole[0]], RD.at[j - 1, whole[0]], s_rd, (0, j - 1), along(2, j)) for j in (2, 1, 3)]

    def sl(o, xx, a, u, rows):
        return (xx, a, u, rows) if o == 1 else (xx, u, a, rows)

    full = slice(None)

    def hop(o, k):
        a, xx = me[o], xk[k]
        plus, minus = along(o, 1), along(o, -1)
        n = (o - 1, k)
        return [
            send(SB.at[sl(o, xx, m4(a + 2), full, first[o])], RB[o].at[xx, :, lo[o]], s_r1, (*n, 0), plus),
            send(SB.at[sl(o, xx, m4(a + 2), full, second[o])], RB[o].at[xx, :, hi[o]], s_r1, (*n, 1), minus),
            send(SB.at[sl(o, xx, m4(a + 1), full, second[o])], RA[o].at[0, xx, :, hi[o]], s_r1, (*n, 2), plus),
            send(SB.at[sl(o, xx, m4(a - 1), full, first[o])], RA[o].at[1, xx, :, lo[o]], s_r1, (*n, 3), minus),
            send(RB[o].at[xx, :, lo[o]], RA[o].at[0, xx, :, lo[o]], s_r1, (*n, 4), plus),
            send(RB[o].at[xx, :, hi[o]], RA[o].at[1, xx, :, hi[o]], s_r1, (*n, 5), minus)]

    hops = {(o, k): hop(o, k) for o in (1, 2) for k in range(4)}
    P2_1 = [[send(SB.at[xk[k], y, m4(z + j), whole[1]], RC1.at[j - 1, xk[k]], s_c1, (k, j - 1), along(2, j))
             for j in (2, 1, 3)] for k in range(4)]
    rel = (2, 1, 3)
    P3_1 = [send(SB.at[xk[k], y, z, whole[1]], RD.at[rel[k] - 1, whole[1]], s_rd, (1, rel[k] - 1), along(0, rel[k]))
            for k in range(3)]
    P2_2 = [send(SB.at[xk[k], :, z, whole[2]], RC2.at[rel[k] - 1], s_c2, (rel[k] - 1,), along(0, rel[k])) for k in range(3)]
    P3_2 = [send(SB.at[x, m4(y + j), z, whole[2]], RD.at[j - 1, whole[2]], s_rd, (2, j - 1), along(1, j)) for j in (2, 1, 3)]

    def start_hops(k):
        for n in range(4):
            for o in (1, 2):
                hops[o, k][n].start()

    def relay_hops(k):
        xx = xk[k]
        for o in (1, 2):
            for e in hops[o, k][:2]:
                e.wait_recv()

            def add(u, o=o):
                a = me[o]
                plus_into(RB[o], (xx, u, lo[o]), (SB, sl(o, xx, m4(a + 1), u, first[o])))
                plus_into(RB[o], (xx, u, hi[o]), (SB, sl(o, xx, m4(a - 1), u, second[o])))

            loop(4, add)
            for e in hops[o, k][4:]:
                e.start()

    def finish_hops(k):
        xx = xk[k]
        for o in (1, 2):
            for e in hops[o, k][2:]:
                e.wait_recv()

            def add(u, o=o):
                plus_into(SB, sl(o, xx, me[o], u, whole[o]), (RA[o], (0, xx, u)), (RA[o], (1, xx, u)))

            loop(4, add)
            for e in (P2_1[k] if o == 1 else P2_2[k:k + 1]):
                e.start()

    def finish_1(k):
        for e in P2_1[k]:
            e.wait_recv()
        plus_into(SB, (xk[k], y, z, whole[1]), *[(RC1, (j, xk[k])) for j in range(3)])
        if k < 3:
            P3_1[k].start()

    def relay_0(r):
        far0[r].wait_recv()
        rows, mine = ((lo, first), (hi, second))[r]

        def add(i):
            plus_into(RB0, (i // 4, i % 4, rows[0]), (SB, (xk[1 + r], i // 4, i % 4, mine[0])))

        loop(16, add)
        relay0[r].start()

    def gw_copy(n):
        m = (n + 4) % 7
        return pltpu.make_async_copy(stage.at[n % 2], gw_out.at[pl.ds(m * 512, 512)], s_out.at[n % 2])

    def gw(n):
        k = pl.ds((n + 4) % 7 * 512, 512)
        if n > 1:
            gw_copy(n - 2).wait()
        out = dot(H[:, :, :, :, k].reshape(1024, 512), T[:, :, :, :, cols_c].reshape(1024, C), ((0,), (0,)))
        out = out + dot(HO[:, :, :, :, k].reshape(1024, 512), GX[...].reshape(1024, C), ((0,), (0,)))
        stage[n % 2] = out.astype(BF)
        gw_copy(n).start()

    HXA = [send(H.at[xx, :, :, :, 2 * C:D], HO.at[xx, :, :, :, 2 * C:D], s_h, (0, xx), sibling) for xx in range(4)]
    HXB = [send(H.at[xx, :, :, :, 0:2 * C], HO.at[xx, :, :, :, 0:2 * C], s_h, (1, xx), sibling) for xx in range(4)]
    GXC = [send(T.at[xx, :, :, :, pl.ds(pl.multiple_of((1 - c) * C, C), C)], GX.at[xx], s_g, (k,), sibling)
           for k, xx in enumerate(xk)]
    cex = [[send(CT.at[a], CR.at[a, k], s_ct, (a, k), along(a, k + 1)) for k in range(3)] for a in range(3)]

    def sum_cross(a):
        for e in cex[a]:
            e.wait()
        CT[a + 1] = CT[a] + CR[a, 0] + CR[a, 1] + CR[a, 2]
        if a < 2:
            for e in cex[a + 1]:
                e.start()

    for k in range(4):
        for n in ((1, 4), (3, 6), (5, 2), (0,))[k]:
            A[n].wait_recv()
        if k == 3:
            local[5].wait()
        for q in range(2):
            grads(2 * xk[k] + q)
        units(xk[k])
        start_hops(k)
        if k == 0:
            for e in far0:
                e.start()
        if k in (1, 2):
            near0[k - 1].start()
        GXC[k].start()
        if k == 1:
            for e in HXA:
                e.start()
        if k == 3:
            for e in A:
                e.wait_send()
            pl.semaphore_signal(s_free, inc=1, device_id=sibling, device_id_type=MESH)
        if k > 0:
            relay_hops(k - 1)
        if k in (1, 2):
            relay_0(k - 1)
        if k > 1:
            finish_hops(k - 2)
    for e in cex[0]:
        e.start()
    finish_1(0)
    pl.semaphore_wait(s_free, 1)
    for e in HXB:
        e.start()
    for e in GXC + HXA:
        e.wait_recv()
    gw(0)
    relay_hops(3)
    finish_hops(2)
    for e in near0 + relay0:
        e.wait_recv()

    def add_0(i):
        plus_into(SB, (x, i // 4, i % 4, whole[0]), (RA0, (0, i // 4, i % 4)), (RA0, (1, i // 4, i % 4)))

    loop(16, add_0)
    for e in P2_0:
        e.start()
    finish_1(1)
    sum_cross(0)
    gw(1)
    finish_hops(3)
    finish_1(2)
    sum_cross(1)
    gw(2)
    for e in P2_0 + P2_2:
        e.wait_recv()

    def add_1(u):
        plus_into(SB, (x, y, u, whole[0]), *[(RC0, (j, u)) for j in range(3)])
        plus_into(SB, (x, u, z, whole[2]), *[(RC2, (j, u)) for j in range(3)])

    loop(4, add_1)
    for e in P3_0 + P3_2:
        e.start()
    for e in HXB:
        e.wait_recv()
    gw(3)
    finish_1(3)
    sum_cross(2)
    gw(4)
    gw(5)
    gw(6)
    b_me = x * 2 + p
    kl_out[...] = (CT[3, pl.ds(b_me, 1), :] - LSE[1, pl.ds(b_me, 1), :]) + LSE[0, pl.ds(b_me, 1), :]
    for e in P3_0 + P3_1 + P3_2:
        e.wait_recv()
    total = SB[x, y, z].astype(F32)
    for k in range(3):
        total = total + RD[k].astype(F32)
    gh_out[...] = total.astype(BF)

    for n in (5, 6):
        gw_copy(n).wait()
    for e in GXC + HXA + HXB:
        e.wait_send()
    for e in far0 + near0 + relay0 + P2_0 + P3_0 + P3_1 + P2_2 + P3_2:
        e.wait_send()
    for k in range(4):
        for e in hops[1, k] + hops[2, k] + P2_1[k]:
            e.wait_send()


def write_out(src, dst, held, sems):
    rows = [pl.ds(n * (D // 14), D // 14) for n in range(14)]
    into = [pltpu.make_async_copy(src.at[r], held.at[r], sems.at[0, n]) for n, r in enumerate(rows)]
    out = [pltpu.make_async_copy(held.at[r], dst.at[r], sems.at[1, n]) for n, r in enumerate(rows)]
    for e in into:
        e.start()
    for a, b in zip(into, out):
        a.wait()
        b.start()
    for e in out:
        e.wait()


def local(hidden, head_weight, teacher_logits, upstream):
    any_ = pl.BlockSpec(memory_space=pl.ANY)
    vmem = pl.BlockSpec(memory_space=pltpu.VMEM)
    dma = pltpu.SemaphoreType.DMA
    scratch = [
        pltpu.VMEM((4, 2, 4, 32, D), BF),
        pltpu.VMEM((4, 2, 4, 32, D), BF),
        pltpu.VMEM((D, 2 * C), BF),
        pltpu.VMEM((4, 2, 4, 32, 2 * C), BF),
        pltpu.VMEM((4, 2, 4, 32, 2 * C), F32),
        pltpu.VMEM((4, 2, 4, 32, C), BF),
        pltpu.VMEM((4, 4, 4, F, 128), BF),
        *[pltpu.VMEM((2, 4, 4, n, 128), BF) for n in COUNT],
        *[pltpu.VMEM((4, 4, n, 128), BF) for n in COUNT],
        *[pltpu.VMEM((3, 4, n, 128), BF) for n in COUNT],
        pltpu.VMEM((3, F, 128), BF),
        pltpu.VMEM((4, 2, 4, 32, 128), F32),
        pltpu.VMEM((4, 2, 4, 32, 128), F32),
        pltpu.VMEM((4, 4, 8, 128), F32),
        pltpu.VMEM((3, 3, 4, 8, 128), F32),
        pltpu.VMEM((4, 8, 128), F32),
        pltpu.VMEM((3, 3, 8, 128), F32),
        pltpu.VMEM((2, 8, 128), F32),
        pltpu.VMEM((4, 128, 128), F32),
        pltpu.VMEM((2, 512, C), BF),
        dma((6,)), dma((2,)), dma((2, 3)), dma((2, 4)), dma((2, 3)), dma((2, 4)), dma((2, 3, 2, 2)), dma((2, 3, 2, 2)),
        dma((2, 7)), dma((2,)), dma((2, 2, 4)), dma((2, 4)), dma((2, 3, 3)), dma((2, 3, 3)), dma((2, 6)), dma((2, 2, 4, 6)),
        dma((2, 3)), dma((2, 4, 3)), dma((2, 3)), dma((2, 3, 3)), dma((2,)), pltpu.SemaphoreType.REGULAR,
    ]
    gh, gw, kl = pl.pallas_call(
        kernel,
        out_shape=[jax.ShapeDtypeStruct((F, 128), BF), jax.ShapeDtypeStruct((D, C), BF),
                   jax.ShapeDtypeStruct((1, 128), F32)],
        in_specs=[any_, any_, any_, vmem],
        out_specs=[vmem, any_, vmem],
        scratch_shapes=scratch,
        compiler_params=pltpu.CompilerParams(collective_id=0, has_side_effects=True, vmem_limit_bytes=64 * 2**20 - 65536),
        cost_estimate=pl.CostEstimate(flops=45 * 10**9, bytes_accessed=60 * 2**20, transcendentals=8 * 2**20),
    )(hidden, head_weight, teacher_logits.reshape(2 * C, C), upstream.reshape(16, 128))
    gw = pl.pallas_call(
        write_out,
        out_shape=jax.ShapeDtypeStruct((D, C), BF),
        in_specs=[any_],
        out_specs=any_,
        scratch_shapes=[pltpu.VMEM((D, C), BF), dma((2, 14))],
        compiler_params=pltpu.CompilerParams(vmem_limit_bytes=60 * 2**20),
        cost_estimate=pl.CostEstimate(flops=0, bytes_accessed=14 * 2**20, transcendentals=0),
    )(gw)
    return gh.T, gw, kl.reshape(128)


def solution(mesh):
    return jax.shard_map(
        local,
        mesh=mesh,
        in_specs=(P("dp", None), P(None, ("dp", "vocab")), P("dp", None, "vocab"), P()),
        out_specs=(P("dp", "vocab"), P(None, ("dp", "vocab")), P("dp")),
        check_vma=False,
    )
```

time: 569 us -> 142 us (0.25)
  blocking collectives: 221 us -> 0 us
  waiting for transfers between devices: 214 us -> 0 us
  Pallas kernels: 0 us -> 140 us
  matrix products: 64.4 us -> 0 us
  local copies, waits for them, and re-layouts: 30.4 us -> 1.17 us
  other arithmetic: 24.2 us -> 0 us
  between operations: 13.8 us -> 0.67 us
    reduce_scatter x1 -> x0, waiting for transfers between devices: 152 us -> none  [local(): lax.psum_scatter(lax.dot_general(grad_logits, head_weight, (((1,), (1,)),...]
    pallas_call x0 -> x2, Pallas kernels: none -> 140 us  [the longest x1 134 us: local(): pl.pallas_call(kernel, out_shape=[jax.ShapeDtypeStruct((F, 128), BF), jax...]
    all_to_all x1 -> x0, blocking collectives: 89.6 us -> none  [local(): lax.all_to_all(teacher_logits, 'dp', split_axis=1, concat_axis=0, tiled=T...]
    pmax x1 -> x0, blocking collectives: 67.2 us -> none  [local(): peak_s, peak_t = lax.pmax((local_s, local_t), ('dp', 'vocab'))]
    dot_general x3 -> x0, matrix products: 64.4 us -> none  [the longest x1 21.8 us: local(): lax.dot_general(gathered, grad_logits, (((0,), (0,)), ((), ())), preferre...]
    psum x1 -> x0, blocking collectives: 63.8 us -> none  [local(): lax.psum((jnp.sum(jnp.exp(student - peak_s[:, None]), axis=1), jnp.sum(ex...]
    unnamed x4 -> x0, waiting for transfers between devices: 46.3 us -> none
    unnamed x11 -> x6, local copies, waits for them, and re-layouts: 21.2 us -> 1.17 us
  transfers between devices with their start and end apart: 3 -> 0, of which waited for: 3 -> 0; matrix products, arithmetic and copies ran while one was open for 9% -> 0% of each run, Pallas kernels for 0% -> 0%
where the time goes in v1:
time: 142 us
  Pallas kernels  140 us (99%)
    pallas_call x1, Pallas kernels, local(): pl.pallas_call(kernel, out_shape=[jax.ShapeDtypeStruct((F, 128), BF), jax...  134 us
    pallas_call x1, Pallas kernels, local(): pl.pallas_call(write_out, out_shape=jax.ShapeDtypeStruct((D, C), BF), in_...  6 us

profile of v1, /device:TPU:2, one launch (start us, length us, event | category | flops | bytes accessed | tf_op | source)
XLA Modules:
  0.0 142.2 jit_solution(12448263412519524286)
XLA Ops:
  0.6 134.4 %shard_map.67 = (bf16[448,128]{1,0:T(8,128)(2,1)}, bf16[3584,1024]{1,0:T(8,128)(2,1)}, f32[1,128]{1,0:T(1,128)}) custom-call(bf16[128,3584]{1,0:T(8,128)(2,1)} %hid.1, bf16[3584,1024]{1,0:T(8,128)(2,1)} %w.1, bf16[2048,1024]{1,0:T(8,128)(2,1)} %bitcast.5, f32[16,128]{1,0:T(8,128)} %bitcast.6), custom_call_target="tpu_custom_call" | custom-call | flops 44999999488 | bytes 62914560 | tf_op jit(solution)/shard_map/pallas_call | solution.py:552
  135.0 0.0 copy-start
  135.0 0.0 copy-start.1
  135.0 6.0 %shard_map.68 = bf16[3584,1024]{1,0:T(8,128)(2,1)} custom-call(bf16[3584,1024]{1,0:T(8,128)(2,1)} %get-tuple-element.7.src), custom_call_target="tpu_custom_call" | custom-call | bytes 14680064 | tf_op jit(solution)/shard_map/pallas_call | solution.py:562
  141.0 0.0 copy-done
  141.1 0.6 copy.9
  141.7 0.0 copy-done.1
  141.7 0.5 copy.10
Async XLA Ops:
  135.0 6.0 %copy-start = (bf16[448,128]{1,0:T(8,128)(2,1)S(1)}, bf16[448,128]{1,0:T(8,128)(2,1)}, u32[]{:S(2)}) copy-start(bf16[448,128]{1,0:T(8,128)(2,1)} %get-tuple-element.6) | copy-start | bytes 344068
  135.0 6.7 %copy-start.1 = (f32[1,128]{1,0:T(1,128)S(1)}, f32[1,128]{1,0:T(1,128)}, u32[]{:S(2)}) copy-start(f32[1,128]{1,0:T(1,128)} %get-tuple-element.8) | copy-start | bytes 1540

commit v2 on v1

--- a/solution.py
+++ b/solution.py
@@ -81,22 +81,17 @@
     cols_c = pl.ds(pl.multiple_of(c * C, C), C)
     X = [send(hid.at[own], H.at[x, p, z], s_x, (i,), along(0, (1, -1, 2)[i])) for i in range(3)]
     A = [send(HO.at[a, b % 2, :, :, 0:2 * C], T.at[x, p], s_a, (k,), da[k]) for k, (a, b) in enumerate(a2a)]
-    Y0 = [send(hid.at[pl.ds(pl.multiple_of(m4(z + k) * 32, 32), 32)], H.at[x, p, m4(z + k)], s_y0, (k,), dyn)
+    Y0 = [send(hid.at[pl.ds(pl.multiple_of(m4(z + k) * 32, 32), 32)], H.at[x, p, m4(z + k)], s_y0, (k,), dyn if k % 2 == 0 else dyl)
           for k in range(4)]
-    low, high = pl.ds(0, 16), pl.ds(16, 16)
     Y1 = [send(H.at[xq[i], p, z], H.at[xq[i], p, z], s_y, (i,), dyn) for i in range(2)]
-    Y1.append(send(H.at[xq[2], p, z, high], H.at[xq[2], p, z, high], s_y, (2,), dyn))
-    YB = [send(H.at[xq[2], p, zz, low], H.at[xq[2], p, zz, low], s_yb, (k,), dyn)
+    YB = [send(H.at[xq[2], p, zz], H.at[xq[2], p, zz], s_yb, (k,), dyn)
           for k, zz in enumerate((z, zq[0], zq[1], m4(z + 2)))]
-    pairs = [(2, 0), (0, 0), (1, 0), (0, 1), (1, 1), (2, 1)]
+    pairs = [(2, 0), (0, 0), (1, 0), (0, 1), (1, 1)]
 
     def piece(i, q, zz):
-        at = H.at[xq[i], (p + q) % 2, zz]
-        return at.at[high] if (i, q) == (2, 1) else at
+        return H.at[xq[i], (p + q) % 2, zz]
 
     def part_of(i, q, zz, r):
-        if (i, q) == (2, 1):
-            return H.at[xq[i], (p + q) % 2, zz, high, r * (D // 2):(r + 1) * (D // 2)]
         return H.at[xq[i], (p + q) % 2, zz, pl.ds(16 * r, 16)]
 
     Z = {(i, q): [send(piece(i, q, z), piece(i, q, z), s_z, (i, q, r), dz[r]) for r in range(2)] for i, q in pairs}
@@ -108,6 +103,11 @@
     for e in X:
         e.start()
     Y0[0].start()
+    Y0[1].start()
+    Y0[3].start()
+    WC.start()
+    for l in local:
+        l.start()
 
     def t_copy(n, slot):
         return pltpu.make_async_copy(
@@ -125,22 +125,16 @@
             t_copy(n + 2, n % 2).start()
         for a in range(16):
             HO[a // 4, (a // 2) % 2, n // 2, pl.ds((n % 2) * 16, 16), pl.ds((a % 2) * C, C)] = moved[a * 16:a * 16 + 16]
-    WC.start()
-    for l in local:
-        l.start()
     local.append(pltpu.make_async_copy(HO.at[x, p, :, :, 0:2 * C], T.at[x, p], s_loc.at[5]))
     local[5].start()
     for i in range(3):
         X[i].wait_recv()
-        Y1[i].start()
-        if i == 2:
-            YB[0].start()
+        (Y1 + YB)[i].start()
         for r in range(2):
             Z[i, 0][r].start()
     for e in A:
         e.start()
-    for k in range(1, 4):
-        Y0[k].start()
+    Y0[2].start()
 
     def teacher(i):
         rows = pl.ds(pl.multiple_of(i * 32, 32), 32)
@@ -167,7 +161,7 @@
 
     ST[0, 2] = jnp.full((8, 128), -1e30, F32)
     ST[0, 3] = jnp.zeros((8, 128), F32)
-    for i in range(3):
+    for i in range(2):
         Y1[i].wait_recv()
         for r in range(2):
             Z[i, 1][r].start()
@@ -204,21 +198,28 @@
         lax.fori_loop(0, 8, stats, 0)
 
     student(z)
-    for i, q in pairs:
+    for i, q in pairs[:4]:
         for r in range(2):
             Z[i, q][r].wait_recv()
-            if (i, q) == (2, 0):
+            if i == 2:
                 YB[1 + r].start()
-            FW[i, q][r].start()
-        if (i, q) == (1, 0):
-            for r in range(2):
-                FW[2, 0][r].wait_recv()
-            YB[3].start()
+    for at in pairs[:3]:
+        for r in range(2):
+            FW[at][r].start()
+    for r in range(2):
+        Z[1, 1][r].wait_recv()
+    for at in pairs[3:]:
+        for r in range(2):
+            FW[at][r].start()
     for k in range(1, 4):
         Y0[k].wait_recv()
     for r in range(2):
         YB[1 + r].wait_recv()
         student(zq[r])
+        if r == 0:
+            for n in range(2):
+                FW[2, 0][n].wait_recv()
+            YB[3].start()
     for i, q in pairs[1:]:
         for r in range(2):
             FW[i, q][r].wait_recv()
@@ -422,6 +423,8 @@
         for q in range(2):
             grads(2 * xk[k] + q)
         units(xk[k])
+        if k > 0:
+            relay_hops(k - 1)
         start_hops(k)
         if k == 0:
             for e in far0:
@@ -436,15 +439,12 @@
             for e in A:
                 e.wait_send()
             pl.semaphore_signal(s_free, inc=1, device_id=sibling, device_id_type=MESH)
-        if k > 0:
-            relay_hops(k - 1)
         if k in (1, 2):
             relay_0(k - 1)
-        if k > 1:
-            finish_hops(k - 2)
+        if k > 2:
+            finish_hops(k - 3)
     for e in cex[0]:
         e.start()
-    finish_1(0)
     pl.semaphore_wait(s_free, 1)
     for e in HXB:
         e.start()
@@ -452,7 +452,8 @@
         e.wait_recv()
     gw(0)
     relay_hops(3)
-    finish_hops(2)
+    finish_hops(1)
+    finish_1(0)
     for e in near0 + relay0:
         e.wait_recv()
 
@@ -462,27 +463,28 @@
     loop(16, add_0)
     for e in P2_0:
         e.start()
+    gw(1)
+    finish_hops(2)
     finish_1(1)
     sum_cross(0)
-    gw(1)
+    gw(2)
     finish_hops(3)
     finish_1(2)
     sum_cross(1)
-    gw(2)
-    for e in P2_0 + P2_2:
-        e.wait_recv()
-
-    def add_1(u):
-        plus_into(SB, (x, y, u, whole[0]), *[(RC0, (j, u)) for j in range(3)])
-        plus_into(SB, (x, u, z, whole[2]), *[(RC2, (j, u)) for j in range(3)])
-
-    loop(4, add_1)
-    for e in P3_0 + P3_2:
-        e.start()
     for e in HXB:
         e.wait_recv()
     gw(3)
     finish_1(3)
+    for e in P2_0 + P2_2:
+        e.wait_recv()
+
+    def add_1(u):
+        plus_into(SB, (x, y, u, whole[0]), *[(RC0, (j, u)) for j in range(3)])
+        plus_into(SB, (x, u, z, whole[2]), *[(RC2, (j, u)) for j in range(3)])
+
+    loop(4, add_1)
+    for e in P3_0 + P3_2:
+        e.start()
     sum_cross(2)
     gw(4)
     gw(5)

time: 142 us -> 141 us (level)
  no operation moved by 1% of the time
where the time goes in v2:
time: 141 us
  Pallas kernels  139 us (99%)
    pallas_call x1, Pallas kernels, local(): pl.pallas_call(kernel, out_shape=[jax.ShapeDtypeStruct((F, 128), BF), jax...  133 us
    pallas_call x1, Pallas kernels, local(): pl.pallas_call(write_out, out_shape=jax.ShapeDtypeStruct((D, C), BF), in_...  6 us

profile of v2, /device:TPU:2, one launch (start us, length us, event | category | flops | bytes accessed | tf_op | source)
XLA Modules:
  0.0 140.9 jit_solution(737393013358376965)
XLA Ops:
  0.6 133.0 %shard_map.67 = (bf16[448,128]{1,0:T(8,128)(2,1)}, bf16[3584,1024]{1,0:T(8,128)(2,1)}, f32[1,128]{1,0:T(1,128)}) custom-call(bf16[128,3584]{1,0:T(8,128)(2,1)} %hid.1, bf16[3584,1024]{1,0:T(8,128)(2,1)} %w.1, bf16[2048,1024]{1,0:T(8,128)(2,1)} %bitcast.5, f32[16,128]{1,0:T(8,128)} %bitcast.6), custom_call_target="tpu_custom_call" | custom-call | flops 44999999488 | bytes 62914560 | tf_op jit(solution)/shard_map/pallas_call | solution.py:554
  133.6 0.0 copy-start
  133.7 0.0 copy-start.1
  133.7 6.0 %shard_map.68 = bf16[3584,1024]{1,0:T(8,128)(2,1)} custom-call(bf16[3584,1024]{1,0:T(8,128)(2,1)} %get-tuple-element.7.src), custom_call_target="tpu_custom_call" | custom-call | bytes 14680064 | tf_op jit(solution)/shard_map/pallas_call | solution.py:564
  139.7 0.0 copy-done
  139.7 0.6 copy.9
  140.3 0.0 copy-done.1
  140.3 0.5 copy.10
Async XLA Ops:
  133.6 6.0 %copy-start = (bf16[448,128]{1,0:T(8,128)(2,1)S(1)}, bf16[448,128]{1,0:T(8,128)(2,1)}, u32[]{:S(2)}) copy-start(bf16[448,128]{1,0:T(8,128)(2,1)} %get-tuple-element.6) | copy-start | bytes 344068
  133.7 6.7 %copy-start.1 = (f32[1,128]{1,0:T(1,128)S(1)}, f32[1,128]{1,0:T(1,128)}, u32[]{:S(2)}) copy-start(f32[1,128]{1,0:T(1,128)} %get-tuple-element.8) | copy-start | bytes 1540
